TPU v7x, 512 devices: a whole 4x4x16 slice. The times are simulated.
512 devices in a mesh: freq: 8 (over x, core), tile: 64 (over z, y).
Axes of the slice: x: 4, y: 4, z: 16, core: 2. Of those that a mesh axis runs over, the one named last changes fastest.
Arguments:
- left_basis: bfloat16 [16, 8192, 2, 1536], P('freq', 'tile'), may hold values from -0.078125 to 0.078125
- right_basis: bfloat16 [16, 8192, 2, 1536], P('freq', 'tile'), may hold values from -0.25 to 0.25
- start_model: float32 [16, 8192, 128], P('freq', 'tile'), may hold values from -3 to 3
- recorded: float32 [16, 8192, 128], P('freq', 'tile'), may hold values from -6 to 6
- tile_ranks: int32 [16, 16], replicated, may hold values from 16 to 96, as said below
- mute_start: int32 [8192, 64], P('tile'), may hold values from 0 to 127
- thresholds: float32 [64], replicated, may hold values from 0.05 to 0.5
Outputs:
- estimate: float32 [16, 8192, 128], P('freq', 'tile')
- misfit: float32 [16, 8192, 128], P('freq', 'tile')
Inputs may be any that keep to these rules, and one draw needn't show every extreme that they name: `tile_ranks`: some tile has rank 96 and some rank 16.
All inputs are finite; a program needn't handle non-finite values.
Results may differ from a plain program's by a relative error of at most 0.013.
Values may be sent and summed in bfloat16 or wider, within the bound.
A program may use at most 64 MiB of HBM per device.

v0:
```python
import math
import jax
import jax.numpy as jnp
from jax import lax
from jax.sharding import PartitionSpec as P

NT = 256
OUTER = 2
STEP_SIZE = 0.5


def phase_table(freq_count):
    sample_index = lax.iota(jnp.int32, NT)[:, None]
    bin_index = lax.iota(jnp.int32, freq_count)[None, :] + NT // 4
    phases = (sample_index * bin_index % NT).astype(jnp.float32) * (2.0 * math.pi / NT)
    return jnp.stack([jnp.cos(phases), -jnp.sin(phases)])


def partials(basis, vector, rank_mask):
    frames = basis.shape[0]
    sources = vector.shape[2] // 2
    inside, rank_slots = rank_mask.shape
    product = jnp.einsum("fnak,fnc->fakc", basis, vector, preferred_element_type=jnp.float32)
    real_part = product[:, 0, :, :sources] + product[:, 1, :, sources:]
    imag_part = product[:, 0, :, sources:] - product[:, 1, :, :sources]
    partial_value = jnp.concatenate([real_part, imag_part], 2).reshape(
        frames, inside, rank_slots, 2 * sources
    )
    partial_value = partial_value * rank_mask[None, :, :, None]
    return partial_value.astype(jnp.bfloat16)


def expand(basis, coefficient):
    frames, height, planes, columns = basis.shape
    inside, share_count, rank_slots, narrow = coefficient.shape[1:]
    blocks = basis.reshape(frames, height, planes, inside, rank_slots)
    product = jnp.einsum(
        "fnajk,fjqkw->fnaqw", blocks, coefficient, preferred_element_type=jnp.float32
    )
    product = product.reshape(frames, height, planes, share_count * narrow)
    sources = share_count * narrow // 2
    real_part = product[:, :, 0, :sources] - product[:, :, 1, sources:]
    imag_part = product[:, :, 0, sources:] + product[:, :, 1, :sources]
    return jnp.concatenate([real_part, imag_part], 2)


def shuffle(partial_value):
    frames, inside, rank_slots, columns = partial_value.shape
    tile_count = lax.axis_size("tile")
    group_size = tile_count // inside
    outgoing = jnp.broadcast_to(
        partial_value[:, :, None], (frames, inside, group_size, rank_slots, columns)
    )
    outgoing = outgoing.reshape(frames, tile_count, rank_slots, columns)
    incoming = lax.all_to_all(outgoing, "tile", split_axis=1, concat_axis=1, tiled=True)
    incoming = incoming.reshape(frames, inside, group_size, rank_slots, columns).astype(jnp.float32)
    return jnp.sum(incoming, 2).astype(jnp.bfloat16)[:, :, None]


def sparsify(estimate, mute_start, thresholds):
    spread = lax.all_to_all(
        estimate.astype(jnp.bfloat16), "freq", split_axis=1, concat_axis=0, tiled=True
    ).astype(estimate.dtype)
    freq_count, rows_here, columns = spread.shape
    sources = columns // 2
    wave_table = phase_table(freq_count)
    stacked = spread.reshape(freq_count, rows_here, 2, sources)
    series = jnp.einsum(
        "atk,knas->nst", wave_table, stacked, precision=lax.Precision.HIGHEST
    ) / math.sqrt(freq_count)
    window = lax.dynamic_slice_in_dim(mute_start, lax.axis_index("freq") * rows_here, rows_here, 0)
    sample_index = lax.iota(jnp.int32, NT)
    series = jnp.where(
        sample_index[None, None, :] >= window[:, :, None], series, jnp.zeros_like(series)
    )
    cutoff = thresholds[None, :, None]
    series = series - jnp.clip(series, -cutoff, cutoff)
    returned = jnp.einsum("nst,atk->knas", series, wave_table, precision=lax.Precision.HIGHEST) * (
        2.0 * math.sqrt(freq_count) / NT
    )
    returned = returned.reshape(freq_count, rows_here, columns)
    return lax.all_to_all(
        returned.astype(jnp.bfloat16), "freq", split_axis=0, concat_axis=1, tiled=True
    ).astype(returned.dtype)


def body(left_basis, right_basis, start_model, recorded, tile_ranks, mute_start, thresholds):
    tile_count = lax.axis_size("tile")
    inside = tile_ranks.shape[0]
    group_size = tile_count // inside
    tile_block = lax.axis_index("tile") // group_size
    levels = lax.iota(jnp.int32, left_basis.shape[3] // inside)
    column_ranks = lax.dynamic_slice_in_dim(tile_ranks, tile_block, 1, 1)
    row_ranks = lax.dynamic_slice_in_dim(tile_ranks, tile_block, 1, 0).reshape(inside, 1)
    right_mask = (levels[None, :] < column_ranks).astype(jnp.float32)
    left_mask = (levels[None, :] < row_ranks).astype(jnp.float32)
    model = start_model
    misfit = recorded
    for outer_step in range(OUTER):
        forward = shuffle(partials(right_basis, model.astype(jnp.bfloat16), right_mask))
        misfit = expand(left_basis, forward) - recorded
        adjoint = shuffle(partials(left_basis, misfit.astype(jnp.bfloat16), left_mask))
        model = model - STEP_SIZE * expand(right_basis, adjoint)
        model = sparsify(model, mute_start, thresholds)
    return (model, misfit)


def solution(mesh):
    return jax.shard_map(
        body,
        mesh=mesh,
        in_specs=(
            P("freq", "tile", None, None),
            P("freq", "tile", None, None),
            P("freq", "tile", None),
            P("freq", "tile", None),
            P(),
            P("tile", None),
            P(),
        ),
        out_specs=(P("freq", "tile", None), P("freq", "tile", None)),
        check_vma=False,
    )
```

profile of v0, /device:TPU:1, one launch (start us, length us, event | category | flops | bytes accessed | tf_op | source)
XLA Modules:
  0.0 716.9 jit_solution(524899450441515643)
XLA Ops:
  1.7 3.7 copy.151
  8.9 2.5 sub.83
  11.4 2.4 fusion
  15.5 2.4 broadcast_in_dim.8
  17.9 19.5 %all-to-all-start = ((bf16[2,64,96,128]{3,2,0,1:T(8,128)(2,1)}), bf16[2,64,96,128]{3,2,0,1:T(8,128)(2,1)}, u32[]{:S(2)}, u32[]{:S(2)}) async-start(bf16[2,64,96,128]{3,2,0,1:T(8,128)(2,1)} %bitcast.221), calls=%async_computation | async-start | bytes 6291456 | tf_op jit(solution)/shard_map/all_to_all | solution.py:55
  37.5 3.7 copy.144
  43.0 134.5 %all-to-all-done = bf16[2,64,96,128]{3,2,0,1:T(8,128)(2,1)} async-done(((bf16[2,64,96,128]{3,2,0,1:T(8,128)(2,1)}), bf16[2,64,96,128]{3,2,0,1:T(8,128)(2,1)}, u32[]{:S(2)}, u32[]{:S(2)}) %all-to-all-start) | async-done | bytes 3145760 | tf_op jit(solution)/shard_map/all_to_all | solution.py:55
  182.4 2.5 add.110
  184.9 2.5 sub.89
  187.4 2.7 fusion.1
  192.5 3.5 broadcast_in_dim.9
  196.1 10.5 %all-to-all-start.1 = ((bf16[2,64,96,128]{3,2,0,1:T(8,128)(2,1)}), bf16[2,64,96,128]{3,2,0,1:T(8,128)(2,1)}, u32[]{:S(2)}, u32[]{:S(2)}) async-start(bf16[2,64,96,128]{3,2,0,1:T(8,128)(2,1)} %bitcast.220), calls=%async_computation.1 | async-start | bytes 6291456 | tf_op jit(solution)/shard_map/all_to_all | solution.py:55
  206.8 138.0 %all-to-all-done.1 = bf16[2,64,96,128]{3,2,0,1:T(8,128)(2,1)} async-done(((bf16[2,64,96,128]{3,2,0,1:T(8,128)(2,1)}), bf16[2,64,96,128]{3,2,0,1:T(8,128)(2,1)}, u32[]{:S(2)}, u32[]{:S(2)}) %all-to-all-start.1) | async-done | bytes 3145760 | tf_op jit(solution)/shard_map/all_to_all | solution.py:55
  348.5 12.1 %all-to-all-start.2 = ((bf16[2,128,128]{2,0,1:T(2,128)(2,1)}), bf16[2,128,128]{2,0,1:T(2,128)(2,1)S(1)}, u32[]{:S(2)}, u32[]{:S(2)}) async-start(bf16[2,128,128]{2,0,1:T(2,128)(2,1)} %copy.156), calls=%async_computation.2 | async-start | bytes 131072 | tf_op jit(solution)/shard_map/all_to_all | solution.py:61
  361.4 4.0 all-to-all-done.2
  368.7 8.0 %all_to_all.77 = bf16[16,16,128]{2,1,0:T(8,128)(2,1)S(1)} all-to-all(bf16[16,16,128]{2,1,0:T(8,128)(2,1)S(1)} %convert_element_type.128), channel_id=1, replica_groups=mesh['freq'=8,'tile'=64] {'freq'}, dimensions={0} | all-to-all | bytes 131072 | tf_op jit(solution)/shard_map/all_to_all | solution.py:82
  381.3 2.4 fusion.2
  386.3 146.4 %all_to_all.78 = bf16[2,64,96,128]{3,2,0,1:T(8,128)(2,1)S(1)} all-to-all(bf16[2,64,96,128]{3,2,0,1:T(8,128)(2,1)S(1)} %bitcast.223), channel_id=1, replica_groups=mesh['freq'=8,'tile'=64] {'tile'}, dimensions={1} | all-to-all | bytes 6291456 | tf_op jit(solution)/shard_map/all_to_all | solution.py:55
  539.1 9.5 %all-to-all-start.5 = ((bf16[2,64,96,128]{3,2,0,1:T(8,128)(2,1)}), bf16[2,64,96,128]{3,2,0,1:T(8,128)(2,1)S(1)}, u32[]{:S(2)}, u32[]{:S(2)}) async-start(bf16[2,64,96,128]{3,2,0,1:T(8,128)(2,1)} %bitcast.222), calls=%async_computation.5 | async-start | bytes 6291456 | tf_op jit(solution)/shard_map/all_to_all | solution.py:55
  548.6 4.9 copy.206
  553.7 133.8 %all-to-all-done.5 = bf16[2,64,96,128]{3,2,0,1:T(8,128)(2,1)S(1)} async-done(((bf16[2,64,96,128]{3,2,0,1:T(8,128)(2,1)}), bf16[2,64,96,128]{3,2,0,1:T(8,128)(2,1)S(1)}, u32[]{:S(2)}, u32[]{:S(2)}) %all-to-all-start.5) | async-done | bytes 3145760 | tf_op jit(solution)/shard_map/all_to_all | solution.py:55
  689.6 14.5 %all_to_all.79 = bf16[2,128,128]{2,0,1:T(2,128)(2,1)S(1)} all-to-all(bf16[2,128,128]{2,0,1:T(2,128)(2,1)S(1)} %copy.174), channel_id=1, replica_groups=mesh['freq'=8,'tile'=64] {'freq'}, dimensions={1} | all-to-all | bytes 131072 | tf_op jit(solution)/shard_map/all_to_all | solution.py:61
  707.3 4.0 all-to-all-start.7
  712.1 4.1 all-to-all-done.7
  (92 shorter events, 43.4 us)
Async XLA Ops:
  0.6 360.0 %copy-start = (s32[128,64]{0,1:T(8,128)S(1)}, s32[128,64]{0,1:T(8,128)}, u32[]{:S(2)}) copy-start(s32[128,64]{0,1:T(8,128)} %param.12) | copy-start | bytes 98308
  0.6 4.8 copy-start.5
  1.7 9.7 %copy-start.6 = (f32[16,96]{1,0:T(8,128)}, f32[16,96]{1,0:T(8,128)S(1)}, u32[]{:S(2)}) copy-start(f32[16,96]{1,0:T(8,128)S(1)} %fusion.65) | copy-start | bytes 18436
  17.9 159.6 %all-to-all-start = ((bf16[2,64,96,128]{3,2,0,1:T(8,128)(2,1)}), bf16[2,64,96,128]{3,2,0,1:T(8,128)(2,1)}, u32[]{:S(2)}, u32[]{:S(2)}) async-start(bf16[2,64,96,128]{3,2,0,1:T(8,128)(2,1)} %bitcast.221), calls=%async_computation | async-start | bytes 6291456 | tf_op jit(solution)/shard_map/all_to_all | solution.py:55
  42.2 138.3 %copy-start.3 = (f32[2,128,128]{1,2,0:T(8,128)}, f32[2,128,128]{1,2,0:T(8,128)S(1)}, u32[]{:S(2)}) copy-start(f32[2,128,128]{1,2,0:T(8,128)S(1)} %copy.148) | copy-start | bytes 393220
  196.1 148.7 %all-to-all-start.1 = ((bf16[2,64,96,128]{3,2,0,1:T(8,128)(2,1)}), bf16[2,64,96,128]{3,2,0,1:T(8,128)(2,1)}, u32[]{:S(2)}, u32[]{:S(2)}) async-start(bf16[2,64,96,128]{3,2,0,1:T(8,128)(2,1)} %bitcast.220), calls=%async_computation.1 | async-start | bytes 6291456 | tf_op jit(solution)/shard_map/all_to_all | solution.py:55
  348.5 16.9 %all-to-all-start.2 = ((bf16[2,128,128]{2,0,1:T(2,128)(2,1)}), bf16[2,128,128]{2,0,1:T(2,128)(2,1)S(1)}, u32[]{:S(2)}, u32[]{:S(2)}) async-start(bf16[2,128,128]{2,0,1:T(2,128)(2,1)} %copy.156), calls=%async_computation.2 | async-start | bytes 131072 | tf_op jit(solution)/shard_map/all_to_all | solution.py:61
  361.4 15.9 %copy-start.9 = (f32[64]{0:T(128)}, f32[64]{0:T(128)S(1)}, u32[]{:S(2)}) copy-start(f32[64]{0:T(128)S(1)} %neg.17) | copy-start | bytes 772
  378.5 2.8 copy-start.7
  533.2 0.9 copy-start.4
  539.1 148.4 %all-to-all-start.5 = ((bf16[2,64,96,128]{3,2,0,1:T(8,128)(2,1)}), bf16[2,64,96,128]{3,2,0,1:T(8,128)(2,1)S(1)}, u32[]{:S(2)}, u32[]{:S(2)}) async-start(bf16[2,64,96,128]{3,2,0,1:T(8,128)(2,1)} %bitcast.222), calls=%async_computation.5 | async-start | bytes 6291456 | tf_op jit(solution)/shard_map/all_to_all | solution.py:55
  687.5 1.4 copy-start.2
  688.9 15.9 %copy-start.8 = (f32[64]{0:T(128)S(1)}, f32[64]{0:T(128)}, u32[]{:S(2)}) copy-start(f32[64]{0:T(128)} %param.13) | copy-start | bytes 772
  688.9 15.9 %copy-start.10 = (f32[64]{0:T(128)S(1)}, f32[64]{0:T(128)}, u32[]{:S(2)}) copy-start(f32[64]{0:T(128)} %copy-done.9) | copy-start | bytes 772
  689.5 27.4 %copy-start.1 = (s32[128,64]{0,1:T(8,128)S(1)}, s32[128,64]{0,1:T(8,128)}, u32[]{:S(2)}) copy-start(s32[128,64]{0,1:T(8,128)} %param.12) | copy-start | bytes 98308
  707.3 8.9 %all-to-all-start.7 = ((bf16[16,16,128]{2,1,0:T(8,128)(2,1)}), bf16[16,16,128]{2,1,0:T(8,128)(2,1)S(1)}, u32[]{:S(2)}, u32[]{:S(2)}) async-start(bf16[16,16,128]{2,1,0:T(8,128)(2,1)} %convert_element_type.136), calls=%async_computation.7 | async-start | bytes 131072 | tf_op jit(solution)/shard_map/all_to_all | solution.py:82
where the time goes:
time: 718 us; the launch traced here: 717 us
  waiting for transfers between devices  414 us (58%)
  blocking collectives  169 us (24%)
  starting transfers between devices  55.6 us (8%)
  local copies, waits for them, and re-layouts  48.7 us (7%)
  other arithmetic  18.9 us (3%)
  matrix products  9.25 us (1%)
    all_to_all x3, waiting for transfers between devices, shuffle(): lax.all_to_all(outgoing, 'tile', split_axis=1, concat_axis=1, tiled=True)  406 us
    all_to_all x1, blocking collectives, shuffle(): lax.all_to_all(outgoing, 'tile', split_axis=1, concat_axis=1, tiled=True)  146 us
    all_to_all x3, starting transfers between devices, shuffle(): lax.all_to_all(outgoing, 'tile', split_axis=1, concat_axis=1, tiled=True)  39.5 us
    all_to_all x1, blocking collectives, sparsify(): lax.all_to_all(estimate.astype(jnp.bfloat16), 'freq', split_axis=1, conca...  14.5 us
  transfers between devices with their start and end apart: 5, of which 5 were waited for; matrix products, arithmetic and copies ran while one was open for 2% of the time, Pallas kernels for 0%

commit v1 on v0

--- a/solution.py
+++ b/solution.py
@@ -52,7 +52,15 @@
         partial_value[:, :, None], (frames, inside, group_size, rank_slots, columns)
     )
     outgoing = outgoing.reshape(frames, tile_count, rank_slots, columns)
-    incoming = lax.all_to_all(outgoing, "tile", split_axis=1, concat_axis=1, tiled=True)
+    incoming = jnp.concatenate(
+        lax.all_to_all(
+            jnp.stack(jnp.split(outgoing, lax.psum(1, axis_name="tile"), 1), 0),
+            axis_name="tile",
+            split_axis=0,
+            concat_axis=0,
+        ),
+        1,
+    )
     incoming = incoming.reshape(frames, inside, group_size, rank_slots, columns).astype(jnp.float32)
     return jnp.sum(incoming, 2).astype(jnp.bfloat16)[:, :, None]
 

time: 718 us -> 842 us (1.17)
  local copies, waits for them, and re-layouts: 48.7 us -> 162 us
    unnamed x27 -> x277, local copies, waits for them, and re-layouts: 10.6 us -> 127 us
  transfers between devices with their start and end apart: 5 -> 5, of which waited for: 5 -> 5; matrix products, arithmetic and copies ran while one was open for 2% -> 1% of each run, Pallas kernels for 0% -> 0%
where the time goes in v1:
time: 842 us; the launch traced here: 840 us
  waiting for transfers between devices  415 us (49%)
  blocking collectives  168 us (20%)
  local copies, waits for them, and re-layouts  162 us (19%)
  starting transfers between devices  55.8 us (7%)
  other arithmetic  24.3 us (3%)
  matrix products  13.1 us (2%)
    all_to_all x3, waiting for transfers between devices, shuffle(): lax.all_to_all(jnp.stack(jnp.split(outgoing, lax.psum(1, axis_name='tile'...  407 us
    all_to_all x1, blocking collectives, shuffle(): lax.all_to_all(jnp.stack(jnp.split(outgoing, lax.psum(1, axis_name='tile'...  147 us
    unnamed x277, local copies, waits for them, and re-layouts  127 us
    all_to_all x3, starting transfers between devices, shuffle(): lax.all_to_all(jnp.stack(jnp.split(outgoing, lax.psum(1, axis_name='tile'...  39.7 us
  transfers between devices with their start and end apart: 5, of which 5 were waited for; matrix products, arithmetic and copies ran while one was open for 1% of the time, Pallas kernels for 0%

profile of v1, /device:TPU:1, one launch (start us, length us, event | category | flops | bytes accessed | tf_op | source)
XLA Modules:
  0.0 840.0 jit_solution(8400216117129333420)
XLA Ops:
  1.7 3.7 copy.1452
  8.9 2.5 sub.83
  11.4 2.4 fusion
  55.9 19.5 %all-to-all-start = ((bf16[64,2,1,96,128]{4,3,1,2,0:T(8,128)(2,1)}), bf16[64,2,1,96,128]{4,3,1,2,0:T(8,128)(2,1)}, u32[]{:S(2)}, u32[]{:S(2)}) async-start(bf16[64,2,1,96,128]{4,3,1,2,0:T(8,128)(2,1)} %constant_dynamic-update-slice_fusion), calls=%async_computation | async-start | bytes 6291456 | tf_op jit(solution)/shard_map/all_to_all | solution.py:56
  75.4 3.7 copy.1445
  81.0 134.5 %all-to-all-done = bf16[64,2,1,96,128]{4,3,1,2,0:T(8,128)(2,1)} async-done(((bf16[64,2,1,96,128]{4,3,1,2,0:T(8,128)(2,1)}), bf16[64,2,1,96,128]{4,3,1,2,0:T(8,128)(2,1)}, u32[]{:S(2)}, u32[]{:S(2)}) %all-to-all-start) | async-done | bytes 3145760 | tf_op jit(solution)/shard_map/all_to_all | solution.py:56
  215.5 3.6 reduce_sum.48
  222.6 2.5 add.110
  225.1 2.5 sub.89
  227.6 2.7 fusion.1
  274.2 10.5 %all-to-all-start.1 = ((bf16[64,2,1,96,128]{4,3,1,2,0:T(8,128)(2,1)}), bf16[64,2,1,96,128]{4,3,1,2,0:T(8,128)(2,1)}, u32[]{:S(2)}, u32[]{:S(2)}) async-start(bf16[64,2,1,96,128]{4,3,1,2,0:T(8,128)(2,1)} %constant_dynamic-update-slice_fusion.64), calls=%async_computation.1 | async-start | bytes 6291456 | tf_op jit(solution)/shard_map/all_to_all | solution.py:56
  285.0 138.0 %all-to-all-done.1 = bf16[64,2,1,96,128]{4,3,1,2,0:T(8,128)(2,1)} async-done(((bf16[64,2,1,96,128]{4,3,1,2,0:T(8,128)(2,1)}), bf16[64,2,1,96,128]{4,3,1,2,0:T(8,128)(2,1)}, u32[]{:S(2)}, u32[]{:S(2)}) %all-to-all-start.1) | async-done | bytes 3145760 | tf_op jit(solution)/shard_map/all_to_all | solution.py:56
  423.0 3.6 reduce_sum.49
  429.0 12.1 %all-to-all-start.2 = ((bf16[2,128,128]{2,0,1:T(2,128)(2,1)}), bf16[2,128,128]{2,0,1:T(2,128)(2,1)S(1)}, u32[]{:S(2)}, u32[]{:S(2)}) async-start(bf16[2,128,128]{2,0,1:T(2,128)(2,1)} %copy.1457), calls=%async_computation.2 | async-start | bytes 131072 | tf_op jit(solution)/shard_map/all_to_all | solution.py:69
  441.8 4.0 all-to-all-done.2
  449.1 8.0 all_to_all.77
  467.8 146.5 %all_to_all.78 = bf16[64,2,1,96,128]{4,3,1,2,0:T(8,128)(2,1)} all-to-all(bf16[64,2,1,96,128]{4,3,1,2,0:T(8,128)(2,1)S(1)} %constant_dynamic-update-slice_fusion.128), channel_id=1, replica_groups=mesh['freq'=8,'tile'=64] {'tile'}, dimensions={0} | all-to-all | bytes 6291456 | tf_op jit(solution)/shard_map/all_to_all | solution.py:56
  614.3 2.6 reduce_sum.50
  660.4 9.7 %all-to-all-start.5 = ((bf16[64,2,1,96,128]{4,3,1,2,0:T(8,128)(2,1)}), bf16[64,2,1,96,128]{4,3,1,2,0:T(8,128)(2,1)S(1)}, u32[]{:S(2)}, u32[]{:S(2)}) async-start(bf16[64,2,1,96,128]{4,3,1,2,0:T(8,128)(2,1)} %constant_dynamic-update-slice_fusion.192), calls=%async_computation.5 | async-start | bytes 6291456 | tf_op jit(solution)/shard_map/all_to_all | solution.py:56
  670.1 4.9 copy.1507
  675.1 134.8 %all-to-all-done.5 = bf16[64,2,1,96,128]{4,3,1,2,0:T(8,128)(2,1)S(1)} async-done(((bf16[64,2,1,96,128]{4,3,1,2,0:T(8,128)(2,1)}), bf16[64,2,1,96,128]{4,3,1,2,0:T(8,128)(2,1)S(1)}, u32[]{:S(2)}, u32[]{:S(2)}) %all-to-all-start.5) | async-done | bytes 3145760 | tf_op jit(solution)/shard_map/all_to_all | solution.py:56
  813.9 13.3 %all_to_all.79 = bf16[2,128,128]{2,0,1:T(2,128)(2,1)S(1)} all-to-all(bf16[2,128,128]{2,0,1:T(2,128)(2,1)S(1)} %copy.1475), channel_id=1, replica_groups=mesh['freq'=8,'tile'=64] {'freq'}, dimensions={1} | all-to-all | bytes 131072 | tf_op jit(solution)/shard_map/all_to_all | solution.py:69
  830.5 4.0 all-to-all-start.7
  835.3 4.1 all-to-all-done.7
  (346 shorter events, 164.7 us)
Async XLA Ops:
  0.6 440.4 %copy-start = (s32[128,64]{0,1:T(8,128)S(1)}, s32[128,64]{0,1:T(8,128)}, u32[]{:S(2)}) copy-start(s32[128,64]{0,1:T(8,128)} %param.12) | copy-start | bytes 98308
  0.6 4.8 copy-start.4
  1.7 9.7 %copy-start.5 = (f32[16,96]{1,0:T(8,128)}, f32[16,96]{1,0:T(8,128)S(1)}, u32[]{:S(2)}) copy-start(f32[16,96]{1,0:T(8,128)S(1)} %fusion.65) | copy-start | bytes 18436
  55.9 159.6 %all-to-all-start = ((bf16[64,2,1,96,128]{4,3,1,2,0:T(8,128)(2,1)}), bf16[64,2,1,96,128]{4,3,1,2,0:T(8,128)(2,1)}, u32[]{:S(2)}, u32[]{:S(2)}) async-start(bf16[64,2,1,96,128]{4,3,1,2,0:T(8,128)(2,1)} %constant_dynamic-update-slice_fusion), calls=%async_computation | async-start | bytes 6291456 | tf_op jit(solution)/shard_map/all_to_all | solution.py:56
  80.2 140.5 %copy-start.2 = (f32[2,128,128]{1,2,0:T(8,128)}, f32[2,128,128]{1,2,0:T(8,128)S(1)}, u32[]{:S(2)}) copy-start(f32[2,128,128]{1,2,0:T(8,128)S(1)} %copy.1449) | copy-start | bytes 393220
  274.2 148.7 %all-to-all-start.1 = ((bf16[64,2,1,96,128]{4,3,1,2,0:T(8,128)(2,1)}), bf16[64,2,1,96,128]{4,3,1,2,0:T(8,128)(2,1)}, u32[]{:S(2)}, u32[]{:S(2)}) async-start(bf16[64,2,1,96,128]{4,3,1,2,0:T(8,128)(2,1)} %constant_dynamic-update-slice_fusion.64), calls=%async_computation.1 | async-start | bytes 6291456 | tf_op jit(solution)/shard_map/all_to_all | solution.py:56
  429.0 16.9 %all-to-all-start.2 = ((bf16[2,128,128]{2,0,1:T(2,128)(2,1)}), bf16[2,128,128]{2,0,1:T(2,128)(2,1)S(1)}, u32[]{:S(2)}, u32[]{:S(2)}) async-start(bf16[2,128,128]{2,0,1:T(2,128)(2,1)} %copy.1457), calls=%async_computation.2 | async-start | bytes 131072 | tf_op jit(solution)/shard_map/all_to_all | solution.py:69
  441.8 15.3 %copy-start.8 = (f32[64]{0:T(128)}, f32[64]{0:T(128)S(1)}, u32[]{:S(2)}) copy-start(f32[64]{0:T(128)S(1)} %neg.17) | copy-start | bytes 772
  457.8 3.9 copy-start.6
  614.3 3.0 copy-start.3
  660.4 149.6 %all-to-all-start.5 = ((bf16[64,2,1,96,128]{4,3,1,2,0:T(8,128)(2,1)}), bf16[64,2,1,96,128]{4,3,1,2,0:T(8,128)(2,1)S(1)}, u32[]{:S(2)}, u32[]{:S(2)}) async-start(bf16[64,2,1,96,128]{4,3,1,2,0:T(8,128)(2,1)} %constant_dynamic-update-slice_fusion.192), calls=%async_computation.5 | async-start | bytes 6291456 | tf_op jit(solution)/shard_map/all_to_all | solution.py:56
  811.6 16.4 %copy-start.7 = (f32[64]{0:T(128)S(1)}, f32[64]{0:T(128)}, u32[]{:S(2)}) copy-start(f32[64]{0:T(128)} %param.13) | copy-start | bytes 772
  811.6 16.4 %copy-start.9 = (f32[64]{0:T(128)S(1)}, f32[64]{0:T(128)}, u32[]{:S(2)}) copy-start(f32[64]{0:T(128)} %copy-done.8) | copy-start | bytes 772
  811.6 28.4 %copy-start.1 = (s32[128,64]{0,1:T(8,128)S(1)}, s32[128,64]{0,1:T(8,128)}, u32[]{:S(2)}) copy-start(s32[128,64]{0,1:T(8,128)} %param.12) | copy-start | bytes 98308
  830.5 8.9 %all-to-all-start.7 = ((bf16[16,16,128]{2,1,0:T(8,128)(2,1)}), bf16[16,16,128]{2,1,0:T(8,128)(2,1)S(1)}, u32[]{:S(2)}, u32[]{:S(2)}) async-start(bf16[16,16,128]{2,1,0:T(8,128)(2,1)} %convert_element_type.136), calls=%async_computation.7 | async-start | bytes 131072 | tf_op jit(solution)/shard_map/all_to_all | solution.py:90
